TPU v7x, 32 devices: a whole 2x2x4 slice. The times are simulated.
32 devices in a mesh: groups: 2 (over x), pool: 16 (over z, y, core).
Axes of the slice: x: 2, y: 2, z: 4, core: 2. Of those that a mesh axis runs over, the one named last changes fastest.
Arguments:
- hidden: bfloat16 [512, 8192], P(('groups', 'pool')), parts along dimension 0, may hold values from -450 to 450
- attention_norm_scale: bfloat16 [8192], replicated, may hold values from 0.25 to 1.75
- query_weight_matrix: bfloat16 [8192, 8192], P(None, 'pool'), may hold values from -0.0625 to 0.0625
- adapter_down_weight: bfloat16 [8192, 4096], P(None, ('groups', 'pool')), parts along dimension 1, may hold values from -0.0625 to 0.0625
- adapter_up_weight: bfloat16 [4096, 8192], P('groups', 'pool'), parts along dimension 0, may hold values from -0.75 to 0.75
- row_adapter_index: int32 [512], P(('groups', 'pool')), parts along dimension 0, may hold values from 0 to 31, as said below
- request_pool_index: int32 [1536], P(('groups', 'pool')), parts along dimension 0, may hold values from 0 to 256, as said below
Outputs:
- query: bfloat16 [512, 8192], P('groups', 'pool'), parts along dimension 0
There are 2 independent parts, one for each index of `groups`. A program takes and returns all parts, laid end to end along the dimension named above; an argument that names none is the same for every part. Nothing has to cross between parts.
Inputs may be any that keep to these rules, and one draw needn't show every extreme that they name: `row_adapter_index`: the adapters p * 2 to (p + 1) * 2 - 1 of one pool index p are named by at most 48 rows in all, and by exactly 48 rows for one p. `request_pool_index`: list p (entries p * 48 to (p + 1) * 48 - 1) holds in increasing order every row whose row_adapter_index lies in p * 2 to (p + 1) * 2 - 1, then 256 in the slots left; one list has no such slot.
All inputs are finite; a program needn't handle non-finite values.
Results may differ from a plain program's by a relative error of at most 0.0054.
Values may be sent and summed in bfloat16 or wider, within the bound.
A program may use at most 64 MiB of HBM per device.

v0:
```python
import jax
import jax.numpy as jnp
from jax import lax
from jax.sharding import PartitionSpec as P

ADAPTER_RANK = 64
ADP_DEV = 2


def rms_scaled(row_values, gain_vec):
    values = row_values.astype(jnp.float32)
    mean_square = jnp.mean(values * values, axis=-1, keepdims=True)
    return (values * lax.rsqrt(mean_square + 1e-05) * gain_vec.astype(jnp.float32)).astype(
        jnp.bfloat16
    )


def local(
    hidden,
    attention_norm_scale,
    query_weight_matrix,
    adapter_down_weight,
    adapter_up_weight,
    row_adapter_index,
    request_pool_index,
):
    owner_index = lax.axis_index("pool")
    whole_rows, whole_ids = (
        lax.all_gather(rms_scaled(hidden, attention_norm_scale), "pool", axis=0, tiled=True),
        lax.all_gather(row_adapter_index, "pool", axis=0, tiled=True),
    )
    total_row_number = whole_rows.shape[0]
    query_output = jnp.dot(whole_rows, query_weight_matrix, preferred_element_type=jnp.float32)
    usable = request_pool_index < total_row_number
    safe_rows = jnp.where(usable, request_pool_index, 0)
    selected_factors = jnp.take(whole_rows, safe_rows, axis=0)
    slot_index = jnp.take(whole_ids, safe_rows, axis=0) - owner_index * ADP_DEV
    paired_factors = jnp.dot(
        selected_factors, adapter_down_weight, preferred_element_type=jnp.float32
    )
    paired_factors = paired_factors.reshape(selected_factors.shape[0], ADP_DEV, ADAPTER_RANK)
    selects = (slot_index[:, None] == jnp.arange(ADP_DEV, dtype=jnp.int32)[None, :]) & usable[
        :, None
    ]
    low_rank = jnp.sum(jnp.where(selects[:, :, None], paired_factors, 0.0), axis=1).astype(
        jnp.bfloat16
    )
    row_iota = jnp.arange(total_row_number, dtype=jnp.int32)
    placement = (row_iota[:, None] == request_pool_index[None, :]).astype(jnp.bfloat16)
    local_terms = jnp.dot(placement, low_rank, preferred_element_type=jnp.float32)
    summed = lax.psum(local_terms.reshape(-1, 2 * ADAPTER_RANK), "pool")
    factor_pair = summed.reshape(total_row_number, ADAPTER_RANK)
    factor_pair = factor_pair.astype(jnp.bfloat16)
    adapter_bank = adapter_up_weight.shape[0] // ADAPTER_RANK
    block_size = min(512, total_row_number)

    def widen_rows(inputs):
        id_block, factor_block = inputs
        onehot = (id_block[:, None] == jnp.arange(adapter_bank, dtype=jnp.int32)[None, :]).astype(
            jnp.bfloat16
        )
        scatter_row_values = (onehot[:, :, None] * factor_block[:, None, :]).reshape(
            block_size, adapter_bank * ADAPTER_RANK
        )
        return jnp.dot(scatter_row_values, adapter_up_weight, preferred_element_type=jnp.float32)

    adapter_update = lax.map(
        widen_rows,
        (whole_ids.reshape(-1, block_size), factor_pair.reshape(-1, block_size, ADAPTER_RANK)),
    )
    adapter_update = adapter_update.reshape(total_row_number, -1)
    return (query_output + adapter_update).astype(jnp.bfloat16)


def solution(mesh):
    return jax.shard_map(
        local,
        mesh=mesh,
        in_specs=(
            P(("groups", "pool"), None),
            P(),
            P(None, "pool"),
            P(None, ("groups", "pool")),
            P("groups", "pool"),
            P(("groups", "pool")),
            P(("groups", "pool")),
        ),
        out_specs=P("groups", "pool"),
        check_vma=False,
    )
```

profile of v0, /device:TPU:0, one launch (start us, length us, event | category | flops | bytes accessed | tf_op | source)
XLA Modules:
  0.0 145.7 jit_solution(13011122125457190889)
XLA Ops:
  6.5 0.0 copy-start
  6.5 0.0 all-gather.2.cloned.1.call-start
  6.5 0.9 convert_element_type.31
  7.4 1.1 fusion.4
  8.5 1.8 %fusion.6 = bf16[16,8192]{1,0:T(8,128)(2,1)} fusion(bf16[16,8192]{1,0:T(8,128)(2,1)} %param.7, f32[8192]{0:T(1024)S(1)} %convert_element_type.31, f32[16]{0:T(128)S(1)} %add_rsqrt_fusion), kind=kLoop, calls=%fused_computation.11 | loop fusion | flops 524288 | bytes 557120 | tf_op jit(solution)/shard_map/convert_element_type | solution.py:13
  10.3 0.0 all-gather.2.cloned.1.call-update
  10.4 1.3 dynamic-slice.2
  12.2 0.9 dynamic-update-slice
  13.1 13.7 %all-reduce = s32[256]{0:T(256)S(1)} all-reduce(s32[256]{0:T(256)S(1)} %dynamic-update-slice), channel_id=1, replica_groups=mesh['groups'=2,'pool'=16] {'pool'}, use_global_device_ids=true, to_apply=%add | all-reduce | flops 256 | bytes 2048
  26.8 0.7 compare_and_fusion
  27.5 0.8 gather_fusion
  28.3 0.1 fusion.11
  28.4 0.0 copy-start.1
  28.4 35.3 %all-gather.2.cloned.1.call-done = bf16[256,8192]{1,0:T(8,128)(2,1)} async-done(((bf16[16,8192]{1,0:T(8,128)(2,1)}), bf16[256,8192]{1,0:T(8,128)(2,1)}) %all-gather.2.cloned.1.call-update) | async-done | bytes 4194320 | tf_op jit(solution)/shard_map/all_gather | solution.py:29
  63.8 4.5 %gather_fusion.1 = bf16[48,8192]{1,0:T(8,128)(2,1)S(1)} fusion(bf16[256,8192]{1,0:T(8,128)(2,1)} %all-gather.2.cloned.1.call-done, s32[1024]{0:T(1024)S(1)} %pad_clamp_fusion), kind=kCustom, calls=%fused_computation.1 | custom fusion | bytes 1573056 | tf_op jit(solution)/shard_map/jit(_take)/gather | solution.py:36
  68.2 2.1 %fusion.1 = f32[48,128]{1,0:T(8,128)S(1)} fusion(bf16[8192,128]{1,0:T(8,128)(2,1)} %param.10, bf16[48,8192]{1,0:T(8,128)(2,1)S(1)} %gather_fusion.1, pred[48]{0:T(512)(128)(4,1)S(1)} %get-tuple-element.13), kind=kOutput, calls=%fused_computation.4 | convolution fusion | flops 101056512 | bytes 2908208 | tf_op jit(solution)/shard_map/dot_general | solution.py:38
  70.4 0.1 reshape.102
  70.5 0.2 select_reduce_fusion
  70.7 0.0 copy-done.1
  70.7 0.1 fusion.8
  70.8 0.1 reshape.103
  70.9 59.2 %psum.7 = bf16[128,128]{1,0:T(8,128)(2,1)S(1)} all-reduce(f32[128,128]{1,0:T(8,128)S(1)} %reshape.103), channel_id=1, replica_groups=mesh['groups'=2,'pool'=16] {'pool'}, use_global_device_ids=true, to_apply=%region_2.3 | all-reduce | flops 16384 | bytes 98304 | tf_op jit(solution)/shard_map/psum | solution.py:51
  130.2 0.1 convert_element_type.36
  130.2 0.1 copy.9
  130.3 0.1 broadcast_multiply_fusion
  130.4 7.0 %fusion.14 = f32[256,512]{1,0:T(8,128)S(1)} fusion(bf16[256,8192]{1,0:T(8,128)(2,1)} %all-gather.2.cloned.1.call-done, bf16[8192,512]{1,0:T(8,128)(2,1)} %param.9), kind=kOutput, calls=%fused_computation.30 | convolution fusion | flops 2147483648 | bytes 13107200 | tf_op jit(solution)/shard_map/dot_general | solution.py:33
  137.4 0.0 copy-done
  137.4 1.4 fusion
  (5 shorter events, 0.0 us)
Async XLA Ops:
  6.5 130.9 %copy-start = (bf16[2048,512]{1,0:T(8,128)(2,1)S(1)}, bf16[2048,512]{1,0:T(8,128)(2,1)}, u32[]{:S(2)}) copy-start(bf16[2048,512]{1,0:T(8,128)(2,1)} %param.11) | copy-start | bytes 6291460
  6.5 57.2 %all-gather.2.cloned.1.call-start = ((), (), s32[]{:S(2)}) async-start(), calls=%async_computation | async-start | bytes 4456448 | tf_op jit(solution)/shard_map/all_gather | solution.py:29
  28.4 42.2 %copy-start.1 = (s32[48]{0:T(128)S(1)}, s32[48]{0:T(128)}, u32[]{:S(2)}) copy-start(s32[48]{0:T(128)} %param.13) | copy-start | bytes 580
Sparse Core Ops, SparseCore 0:
  10.5 53.2 all-gather.1
where the time goes:
time: 146 us
  blocking collectives  73 us (50%)
  waiting for transfers between devices  35.4 us (24%)
  between operations  14.1 us (10%)
  matrix products  10.7 us (7%)
  local copies, waits for them, and re-layouts  7.74 us (5%)
  other arithmetic  4.79 us (3%)
    psum x1, blocking collectives, local(): summed = lax.psum(local_terms.reshape(-1, 2 * ADAPTER_RANK), 'pool')  59.2 us
    all_gather x1, waiting for transfers between devices, local(): lax.all_gather(rms_scaled(hidden, attention_norm_scale), 'pool', axis=0,...  35.3 us
    unnamed x1, blocking collectives  13.7 us
    dot_general x1, matrix products, local(): jnp.dot(whole_rows, query_weight_matrix, preferred_element_type=jnp.float32)  6.98 us
    gather x1, local copies, waits for them, and re-layouts, local(): selected_factors = jnp.take(whole_rows, safe_rows, axis=0)  4.47 us
  transfers between devices with their start and end apart: 1, of which 1 were waited for; matrix products, arithmetic and copies ran while one was open for 3% of the time, Pallas kernels for 0%

commit v1 on v0

v1 whole, which is shorter than its diff:
```python
import functools

import jax
import jax.numpy as jnp
from jax import lax
from jax.experimental import pallas as pl
from jax.experimental.pallas import tpu as pltpu
from jax.sharding import PartitionSpec as P

ADAPTER_RANK = 64
ADP_DEV = 2
SLOTS = 64
HALF = SLOTS // 2
CHUNKS = 8
AHEAD = 2
MESH = pl.DeviceIdType.MESH
F32, BF16 = jnp.float32, jnp.bfloat16


def each(n, body):
    if n <= 8:
        for i in range(n):
            body(i)
    else:

        def step(i, carry):
            body(i)
            return carry

        lax.fori_loop(0, n, step, 0)


def kernel(
    nz, ny, h_hbm, g_ref, w_hbm, d_hbm, u_hbm, ids_ref, list_ref, out_ref,
    x, w, d, u, h, acc, accd, meta, comp, expand, idcol, wide,
    h_sem, w_sem, d_sem, u_sem, z_send, y_send, s_send, recv, m_send, m_recv, c_send, c_recv,
):
    pool = nz * ny * 2
    block, width = h_hbm.shape
    rows = block * pool
    kc = width // CHUNKS
    tile = min(rows, 256)
    me = lax.axis_index("pool")
    c = lax.rem(me, 2)
    y = lax.rem(me // 2, ny)
    z = me // (2 * ny)

    def pid(zz, yy, cc):
        return (zz * ny + yy) * 2 + cc

    load_h = pltpu.make_async_copy(h_hbm, h, h_sem)
    load_h.start()

    barrier = pltpu.get_barrier_semaphore()

    def greet(i):
        pl.semaphore_signal(
            barrier, inc=1, device_id={"pool": lax.rem(me + 1 + i, pool)}, device_id_type=MESH
        )

    each(pool - 1, greet)

    mine8 = pl.ds(pl.multiple_of(me * 8, 8), 8)
    meta[mine8, :] = jnp.full((8, 128), -1, jnp.int32)
    meta[pl.ds(me * 8, 1), pl.ds(0, block)] = ids_ref[...].reshape(1, block)
    entries = list_ref.shape[0]
    meta[pl.ds(me * 8 + 1, 1), pl.ds(0, entries)] = list_ref[...].reshape(1, entries)

    def cols(k):
        return pl.ds(pl.multiple_of(k * kc, kc), kc)

    def load_w(k):
        return pltpu.make_async_copy(w_hbm.at[cols(k), :], w.at[cols(k), :], w_sem.at[k])

    def load_d(k):
        return pltpu.make_async_copy(d_hbm.at[cols(k), :], d.at[cols(k), :], d_sem.at[k])

    load_u = pltpu.make_async_copy(u_hbm, u, u_sem)

    load_h.wait()
    for k in range(CHUNKS):
        load_d(k).start()
        load_w(k).start()
    load_u.start()

    total = jnp.zeros((block, 128), F32)
    for k in range(CHUNKS):
        v = h[:, k * kc : (k + 1) * kc].astype(F32)
        v = v * v
        for j in range(kc // 128):
            total = total + v[:, j * 128 : (j + 1) * 128]
    mean = jnp.sum(total, axis=1, keepdims=True) / width
    scale = lax.rsqrt(mean + 1e-05)
    mine = pl.ds(pl.multiple_of(me * block, block), block)
    for k in range(CHUNKS):
        v = h[:, k * kc : (k + 1) * kc].astype(F32)
        g = g_ref[:, k * kc : (k + 1) * kc].astype(F32)
        x[mine, k * kc : (k + 1) * kc] = (v * scale * g).astype(BF16)

    pl.semaphore_wait(barrier, pool - 1)

    def piece(src, k):
        return x.at[pl.ds(pl.multiple_of(src * block, block), block), cols(k)]

    def push(src, k, sem, target):
        return pltpu.make_async_remote_copy(
            src_ref=piece(src, k),
            dst_ref=piece(src, k),
            send_sem=sem,
            recv_sem=recv.at[k, src],
            device_id={"pool": target},
            device_id_type=MESH,
        )

    def to_z(k, i):
        zz = lax.rem(z + 1 + i, nz)
        return push(me, k, z_send.at[k, i], pid(zz, y, c))

    def to_y(k, zz, i):
        yy = lax.rem(y + 1 + i, ny)
        return push(pid(zz, y, c), k, y_send.at[k, zz * max(ny - 1, 1) + i], pid(z, yy, c))

    def to_s(k, zz, yy):
        return push(pid(zz, yy, c), k, s_send.at[k, zz * ny + yy], pid(z, y, 1 - c))

    def arrived(k, src):
        push(src, k, z_send.at[0, 0], pid(z, y, 1 - c)).wait_recv()

    def own(k):
        each(ny - 1, lambda i: to_y(k, z, i).start())
        each(nz - 1, lambda i: to_z(k, i).start())
        to_s(k, z, y).start()

    for k in range(AHEAD):
        own(k)

    def tell(i):
        q = lax.rem(me + 1 + i, pool)
        return pltpu.make_async_remote_copy(
            src_ref=meta.at[mine8, :],
            dst_ref=meta.at[mine8, :],
            send_sem=m_send.at[i],
            recv_sem=m_recv.at[me],
            device_id={"pool": q},
            device_id_type=MESH,
        )

    each(pool - 1, lambda i: tell(i).start())

    acc[...] = jnp.zeros_like(acc)
    accd[...] = jnp.zeros_like(accd)

    def down(k):
        load_d(k).wait()

        def part(t):
            at = pl.ds(pl.multiple_of(t * tile, tile), tile)
            accd[at, :] += jnp.dot(x[at, cols(k)], d[cols(k), :], preferred_element_type=F32)

        each(rows // tile, part)

    def base(k):
        load_w(k).wait()

        def part(t):
            at = pl.ds(pl.multiple_of(t * tile, tile), tile)
            acc[at, :] += jnp.dot(x[at, cols(k)], w[cols(k), :], preferred_element_type=F32)

        each(rows // tile, part)

    def step(i, carry):
        @pl.when(i + AHEAD < CHUNKS)
        def _():
            own(i + AHEAD)

        @pl.when(i < CHUNKS)
        def _():
            def from_z(j):
                zz = lax.rem(z + 1 + j, nz)
                arrived(i, pid(zz, y, c))
                each(ny - 1, lambda t: to_y(i, zz, t).start())
                to_s(i, zz, y).start()

            each(nz - 1, from_z)

        @pl.when((i >= 1) & (i <= CHUNKS))
        def _():
            def from_y(t):
                yy = lax.rem(y + 1 + t, ny)

                def at_z(j):
                    zz = lax.rem(z + j, nz)
                    arrived(i - 1, pid(zz, yy, c))
                    to_s(i - 1, zz, yy).start()

                each(nz, at_z)

            each(ny - 1, from_y)

        @pl.when(i >= 2)
        def _():
            each(nz * ny, lambda q: arrived(i - 2, q * 2 + 1 - c))
            down(i - 2)

            @pl.when(i - 2 < CHUNKS - 1)
            def _():
                base(i - 2)

        @pl.when(i == 1)
        def _():
            tables()

        return carry

    def tables():
        def got(i):
            q = lax.rem(me + 1 + i, pool)
            at = pl.ds(pl.multiple_of(q * 8, 8), 8)
            pltpu.make_async_remote_copy(
                src_ref=meta.at[at, :], dst_ref=meta.at[at, :], send_sem=m_send.at[0],
                recv_sem=m_recv.at[q], device_id={"pool": q}, device_id_type=MESH,
            ).wait_recv()

        each(pool - 1, got)
        lane = lax.broadcasted_iota(jnp.int32, (block, 128), 1)
        sub = lax.broadcasted_iota(jnp.int32, (block, 128), 0)

        def ids(q):
            row = meta[pl.ds(q * 8, 1), :]
            col = jnp.sum(jnp.where(lane == sub, row, 0), axis=1, keepdims=True)
            idcol[pl.ds(pl.multiple_of(q * block, block), block), :] = jnp.broadcast_to(
                col, (block, 128)
            )

        each(pool, ids)

        def quad(q):
            parts = [meta[pl.ds((q * 4 + s) * 8 + 1, 1), :] for s in range(4)]
            for half in range(2):
                line = jnp.concatenate([t[:, half * HALF : (half + 1) * HALF] for t in parts], axis=1)

                def part(t):
                    at = pl.ds(pl.multiple_of(t * tile, tile), tile)
                    row = lax.broadcasted_iota(jnp.int32, (tile, 128), 0) + t * tile
                    expand[half, at, pl.ds(pl.multiple_of(q * 128, 128), 128)] = jnp.where(
                        row == line, 1.0, 0.0
                    ).astype(BF16)

                each(rows // tile, part)

        each(pool // 4, quad)

    lax.fori_loop(0, CHUNKS + 2, step, 0)

    own_list = meta[pl.ds(me * 8 + 1, 1), :]
    eye = lax.broadcasted_iota(jnp.int32, (SLOTS, 128), 0) == lax.broadcasted_iota(
        jnp.int32, (SLOTS, 128), 1
    )
    own_col = jnp.sum(jnp.where(eye, own_list, 0), axis=1, keepdims=True)
    pick = jnp.where(
        own_col == lax.broadcasted_iota(jnp.int32, (SLOTS, rows), 1), 1.0, 0.0
    ).astype(BF16)
    low = jnp.dot(pick, accd[...].astype(BF16), preferred_element_type=F32)
    picked = jnp.dot(pick, idcol[...].astype(F32).astype(BF16), preferred_element_type=F32)
    slot = picked - (me * ADP_DEV).astype(F32)
    lane = lax.broadcasted_iota(jnp.int32, (SLOTS, 128), 1)
    low = jnp.where(slot == (lane // ADAPTER_RANK).astype(F32), low, 0.0)
    low = low[:, :ADAPTER_RANK] + low[:, ADAPTER_RANK:]
    mine_c = pl.ds(pl.multiple_of(me * HALF, HALF), HALF)
    comp[mine_c, :] = jnp.concatenate([low[:HALF], low[HALF:]], axis=1).astype(BF16)

    def share(i):
        return pltpu.make_async_remote_copy(
            src_ref=comp.at[mine_c, :],
            dst_ref=comp.at[mine_c, :],
            send_sem=c_send.at[i],
            recv_sem=c_recv.at[me],
            device_id={"pool": lax.rem(me + 1 + i, pool)},
            device_id_type=MESH,
        )

    each(pool - 1, lambda i: share(i).start())
    base(CHUNKS - 1)
    load_u.wait()

    def got(i):
        q = lax.rem(me + 1 + i, pool)
        at = pl.ds(pl.multiple_of(q * HALF, HALF), HALF)
        pltpu.make_async_remote_copy(
            src_ref=comp.at[at, :], dst_ref=comp.at[at, :], send_sem=c_send.at[0],
            recv_sem=c_recv.at[q], device_id={"pool": q}, device_id_type=MESH,
        ).wait_recv()

    each(pool - 1, got)

    def finish(t):
        at = pl.ds(pl.multiple_of(t * tile, tile), tile)
        first = jnp.dot(expand[0, at, :], comp[...], preferred_element_type=F32)
        second = jnp.dot(expand[1, at, :], comp[...], preferred_element_type=F32)
        factor = first[:, :ADAPTER_RANK] + second[:, ADAPTER_RANK:]
        pair = jnp.concatenate([factor, factor], axis=1).astype(BF16).astype(F32)
        ids = idcol[at, :] - lax.broadcasted_iota(jnp.int32, (tile, 128), 1) // ADAPTER_RANK

        def spread(q):
            wide[:, pl.ds(pl.multiple_of(q * 128, 128), 128)] = jnp.where(
                ids == q * ADP_DEV, pair, 0.0
            ).astype(BF16)

        bank = u.shape[0] // 128
        for q in range(bank):
            spread(q)
        delta = jnp.dot(wide[...], u[...], preferred_element_type=F32)
        out_ref[at, :] = (acc[at, :] + delta).astype(BF16)

    each(rows // tile, finish)

    def done(k):
        each(nz - 1, lambda i: to_z(k, i).wait_send())
        for i in range(ny - 1):
            each(nz, lambda zz: to_y(k, zz, i).wait_send())
        for yy in range(ny):
            each(nz, lambda zz: to_s(k, zz, yy).wait_send())

    lax.fori_loop(0, CHUNKS, lambda k, t: (done(k), t)[1], 0)
    each(pool - 1, lambda i: tell(i).wait_send())
    each(pool - 1, lambda i: share(i).wait_send())


def local(nz, ny, hidden, gain, weight, down, up, ids, requests):
    pool = nz * ny * 2
    block, width = hidden.shape
    rows = block * pool
    n = weight.shape[1]
    tile = min(rows, 256)
    dma = pltpu.SemaphoreType.DMA
    vm = pl.BlockSpec(memory_space=pltpu.VMEM)
    hbm = pl.BlockSpec(memory_space=pl.ANY)
    return pl.pallas_call(
        functools.partial(kernel, nz, ny),
        out_shape=jax.ShapeDtypeStruct((rows, n), BF16),
        in_specs=[hbm, vm, hbm, hbm, hbm, vm, vm],
        out_specs=vm,
        scratch_shapes=[
            pltpu.VMEM((rows, width), BF16),
            pltpu.VMEM(weight.shape, BF16),
            pltpu.VMEM(down.shape, BF16),
            pltpu.VMEM(up.shape, BF16),
            pltpu.VMEM((block, width), BF16),
            pltpu.VMEM((rows, n), F32),
            pltpu.VMEM((rows, down.shape[1]), F32),
            pltpu.VMEM((pool * 8, 128), jnp.int32),
            pltpu.VMEM((pool * HALF, 128), BF16),
            pltpu.VMEM((2, rows, pool * HALF), BF16),
            pltpu.VMEM((rows, 128), jnp.int32),
            pltpu.VMEM((tile, up.shape[0]), BF16),
            dma,
            dma((CHUNKS,)),
            dma((CHUNKS,)),
            dma,
            dma((CHUNKS, nz)),
            dma((CHUNKS, nz * max(ny - 1, 1))),
            dma((CHUNKS, nz * ny)),
            dma((CHUNKS, pool)),
            dma((pool,)),
            dma((pool,)),
            dma((pool,)),
            dma((pool,)),
        ],
        compiler_params=pltpu.CompilerParams(
            collective_id=0, has_side_effects=True, vmem_limit_bytes=56 * 1024 * 1024
        ),
    )(hidden, gain.reshape(1, -1), weight, down, up, ids, requests)


def solution(mesh):
    pool = mesh.shape["pool"]
    ny = 2 if pool == 16 else 1
    nz = pool // (2 * ny)
    return jax.shard_map(
        functools.partial(local, nz, ny),
        mesh=mesh,
        in_specs=(
            P(("groups", "pool"), None),
            P(),
            P(None, "pool"),
            P(None, ("groups", "pool")),
            P("groups", "pool"),
            P(("groups", "pool")),
            P(("groups", "pool")),
        ),
        out_specs=P("groups", "pool"),
        check_vma=False,
    )
```

time: 146 us -> 52.2 us (0.36)
  blocking collectives: 73 us -> 0 us
  Pallas kernels: 0 us -> 48.8 us
  waiting for transfers between devices: 35.4 us -> 0 us
  between operations: 14.1 us -> 0.01 us
  matrix products: 10.7 us -> 0 us
  other arithmetic: 4.79 us -> 0 us
  local copies, waits for them, and re-layouts: 7.74 us -> 3.02 us
    psum x1 -> x0, blocking collectives: 59.2 us -> none  [local(): summed = lax.psum(local_terms.reshape(-1, 2 * ADAPTER_RANK), 'pool')]
    pallas_call x0 -> x1, Pallas kernels: none -> 48.8 us  [local(): pl.pallas_call(functools.partial(kernel, nz, ny), out_shape=jax.ShapeDtyp...]
    all_gather x1 -> x0, waiting for transfers between devices: 35.3 us -> none  [local(): lax.all_gather(rms_scaled(hidden, attention_norm_scale), 'pool', axis=0,...]
    unnamed x1 -> x0, blocking collectives: 13.7 us -> none
    dot_general x4 -> x0, matrix products: 10.7 us -> none  [the longest x1 6.98 us: local(): jnp.dot(whole_rows, query_weight_matrix, preferred_element_type=jnp.float32)]
    gather x2 -> x0, local copies, waits for them, and re-layouts: 5.27 us -> none  [the longest x1 4.47 us: local(): selected_factors = jnp.take(whole_rows, safe_rows, axis=0)]
    convert_element_type x3 -> x0, other arithmetic: 2.67 us -> none  [the longest x1 1.79 us: rms_scaled(): (values * lax.rsqrt(mean_square + 1e-05) * gain_vec.astype(jnp.float32))....]
  transfers between devices with their start and end apart: 1 -> 0, of which waited for: 1 -> 0; matrix products, arithmetic and copies ran while one was open for 3% -> 0% of each run, Pallas kernels for 0% -> 0%
where the time goes in v1:
time: 52.2 us; the launch traced here: 51.9 us
  Pallas kernels  48.8 us (93%)
  local copies, waits for them, and re-layouts  3.02 us (6%)
    pallas_call x1, Pallas kernels, local(): pl.pallas_call(functools.partial(kernel, nz, ny), out_shape=jax.ShapeDtyp...  48.8 us
    unnamed x1, local copies, waits for them, and re-layouts  1.67 us
    reshape x1, local copies, waits for them, and re-layouts, local(): gain.reshape(1, -1)  1.35 us

profile of v1, /device:TPU:0, one launch (start us, length us, event | category | flops | bytes accessed | tf_op | source)
XLA Modules:
  0.0 51.9 jit_solution(5675457804467182439)
XLA Ops:
  0.0 1.3 %reshape.3.g_ref = bf16[1,8192]{1,0:T(2,128)(2,1)} reshape(bf16[8192]{0:T(1024)(128)(2,1)} %param.8) | data formatting | bytes 32768 | tf_op jit(solution)/shard_map/reshape | solution.py:372
  1.4 48.8 %shard_map.73 = bf16[256,512]{1,0:T(8,128)(2,1)} custom-call(bf16[16,8192]{1,0:T(8,128)(2,1)} %h_hbm.1, bf16[1,8192]{1,0:T(2,128)(2,1)} %reshape.3.g_ref, bf16[8192,512]{1,0:T(8,128)(2,1)} %w_hbm.1, bf16[8192,128]{1,0:T(8,128)(2,1)} %d_hbm.1, bf16[2048,512]{1,0:T(8,128)(2,1)} %u_hbm.1, s32[16]{0:T(128)} %ids_ref.1, s32[48]{0:T(128)} %list_ref.1), custom_call_target="tpu_custom_call" | custom-call | tf_op jit(solution)/shard_map/pallas_call | solution.py:338
  50.2 1.7 %copy.9 = bf16[256,512]{1,0:T(8,128)(2,1)} copy(bf16[256,512]{1,0:T(8,128)(2,1)} %shard_map.73) | data formatting | bytes 524288

commit v2 on v1

v2 whole, which is shorter than its diff:
```python
import functools

import jax
import jax.numpy as jnp
from jax import lax
from jax.experimental import pallas as pl
from jax.experimental.pallas import tpu as pltpu
from jax.sharding import PartitionSpec as P

ADAPTER_RANK = 64
ADP_DEV = 2
SLOTS = 64
HALF = SLOTS // 2
CHUNKS = 8
AHEAD = 3
AHEAD_Y = 3
LAG_Y = 2
LAG = 3
MESH = pl.DeviceIdType.MESH
F32, BF16 = jnp.float32, jnp.bfloat16


def each(n, body):
    if n <= 8:
        for i in range(n):
            body(i)
    else:

        def step(i, carry):
            body(i)
            return carry

        lax.fori_loop(0, n, step, 0)


def kernel(
    nz, ny, h_hbm, g_hbm, w_hbm, d_hbm, u_hbm, ids_ref, list_ref, out_ref,
    x, w, d, u, h, g, acc, accd, meta, comp, expand, idcol, wide,
    h_sem, g_sem, w_sem, d_sem, u_sem, z_send, y_send, s_send, recv, s_recv,
    m_send, m_recv, c_send, c_recv,
):
    pool = nz * ny * 2
    lines = nz * ny
    block, width = h_hbm.shape
    rows = block * pool
    kc = width // CHUNKS
    tile = min(rows, 256)
    me = lax.axis_index("pool")
    c = lax.rem(me, 2)
    y = lax.rem(me // 2, ny)
    z = me // (2 * ny)

    def pid(zz, yy, cc):
        return (zz * ny + yy) * 2 + cc

    def place(zz, yy, cc):
        return (cc * ny + yy) * nz + zz

    def row_of(b):
        at = b // block
        zz, yy, cc = lax.rem(at, nz), lax.rem(at // nz, ny), at // lines
        return pid(zz, yy, cc) * block + lax.rem(b, block)

    here = place(z, y, c)

    def to(sem, recv_sem, src, target):
        return pltpu.make_async_remote_copy(
            src_ref=src, dst_ref=src, send_sem=sem, recv_sem=recv_sem,
            device_id={"pool": target}, device_id_type=MESH,
        )

    load_h = pltpu.make_async_copy(h_hbm, h, h_sem)
    load_g = pltpu.make_async_copy(g_hbm, g, g_sem)
    load_h.start()
    load_g.start()

    barrier = pltpu.get_barrier_semaphore()

    def greet(q):
        pl.semaphore_signal(barrier, inc=1, device_id={"pool": q}, device_id_type=MESH)

    greet(pid(z, y, 1 - c))
    each(ny - 1, lambda i: greet(pid(z, lax.rem(y + 1 + i, ny), c)))
    each(nz - 1, lambda i: greet(pid(lax.rem(z + 1 + i, nz), y, c)))

    mine8 = pl.ds(pl.multiple_of(here * 8, 8), 8)
    meta[mine8, :] = jnp.full((8, 128), -1, jnp.int32)
    meta[pl.ds(here * 8, 1), pl.ds(0, block)] = ids_ref[...].reshape(1, block)
    entries = list_ref.shape[0]
    meta[pl.ds(here * 8 + 1, 1), pl.ds(0, entries)] = list_ref[...].reshape(1, entries)

    def cols(k):
        return pl.ds(pl.multiple_of(k * kc, kc), kc)

    def load_w(k):
        return pltpu.make_async_copy(w_hbm.at[cols(k), :], w.at[cols(k), :], w_sem.at[k])

    def load_d(k):
        return pltpu.make_async_copy(d_hbm.at[cols(k), :], d.at[cols(k), :], d_sem.at[k])

    load_u = pltpu.make_async_copy(u_hbm, u, u_sem)

    load_h.wait()
    load_g.wait()
    for k in range(CHUNKS):
        load_d(k).start()
        load_w(k).start()
    load_u.start()

    total = jnp.zeros((block, 128), F32)
    for k in range(CHUNKS):
        v = h[:, k * kc : (k + 1) * kc].astype(F32)
        v = v * v
        for j in range(kc // 128):
            total = total + v[:, j * 128 : (j + 1) * 128]
    mean = jnp.sum(total, axis=1, keepdims=True) / width
    scale = lax.rsqrt(mean + 1e-05)
    mine = pl.ds(pl.multiple_of(here * block, block), block)
    for k in range(CHUNKS):
        v = h[:, k * kc : (k + 1) * kc].astype(F32)
        gain = g[k * kc : (k + 1) * kc].astype(F32).reshape(1, kc)
        x[mine, k * kc : (k + 1) * kc] = (v * scale * gain).astype(BF16)

    pl.semaphore_wait(barrier, nz + ny - 1)

    def piece(at, k, count=1):
        size = block * count
        return x.at[pl.ds(pl.multiple_of(at * block, size), size), cols(k)]

    near = nz == 4

    def far(zz):
        return (zz - z == 3) | (z - zz == 3)

    def to_z(k, i):
        zz = lax.rem(z + 1 + i, nz)
        return to(z_send.at[k, i], recv.at[k, here], piece(here, k), pid(zz, y, c))

    def z_sends(k, act):
        def one(i):
            if near:

                @pl.when(jnp.logical_not(far(lax.rem(z + 1 + i, nz))))
                def _():
                    act(to_z(k, i))
            else:
                act(to_z(k, i))

        each(nz - 1, one)

    def relay(k, act):
        @pl.when((z == 1) | (z == 2))
        def _():
            at = place(6 - 3 * z, y, c)
            act(to(z_send.at[k, nz - 1], recv.at[k, at], piece(at, k), pid(3 * z - 3, y, c)))

    def to_y(k, zz, i):
        at = place(zz, y, c)
        yy = lax.rem(y + 1 + i, ny)
        return to(y_send.at[k, zz * max(ny - 1, 1) + i], recv.at[k, at], piece(at, k), pid(z, yy, c))

    def to_s(k, yy):
        at = place(0, yy, c)
        return to(s_send.at[k, yy], s_recv.at[k, yy], piece(at, k, nz), pid(z, y, 1 - c))

    def arrived(k, at):
        to(z_send.at[0, 0], recv.at[k, at], piece(at, k), pid(z, y, 1 - c)).wait_recv()

    def from_s(k, yy):
        at = place(0, yy, 1 - c)
        to(s_send.at[0, 0], s_recv.at[k, yy], piece(at, k, nz), pid(z, y, 1 - c)).wait_recv()

    def own_y(k):
        each(ny - 1, lambda i: to_y(k, z, i).start())

    def own_z(k):
        z_sends(k, lambda t: t.start())

    for k in range(max(AHEAD, AHEAD_Y)):
        if k < AHEAD:
            own_z(k)
        if k < AHEAD_Y:
            own_y(k)

    acc[...] = jnp.zeros_like(acc)
    accd[...] = jnp.zeros_like(accd)

    def spread_to(buf, size, sem, recv_sem, i):
        q = lax.rem(here - c * lines + 1 + i, lines)
        at = pl.ds(pl.multiple_of(here * size, size), size)
        return to(
            sem.at[i], recv_sem.at[here], buf.at[at, :], pid(lax.rem(q, nz), q // nz, c)
        )

    def spread_from(buf, size, sem, recv_sem, i):
        q = c * lines + lax.rem(here - c * lines + 1 + i, lines)
        at = pl.ds(pl.multiple_of(q * size, size), size)
        to(sem.at[0], recv_sem.at[q], buf.at[at, :], pid(z, y, 1 - c)).wait_recv()

    def across(buf, size, sem, recv_sem, cc):
        at = pl.ds(pl.multiple_of(cc * lines * size, lines * size), lines * size)
        return to(sem.at[lines], recv_sem.at[pool], buf.at[at, :], pid(z, y, 1 - c))

    telling = (meta, 8, m_send, m_recv)
    sharing = (comp, HALF, c_send, c_recv)

    def down(k):
        load_d(k).wait()

        def part(t):
            at = pl.ds(pl.multiple_of(t * tile, tile), tile)
            accd[at, :] += jnp.dot(x[at, cols(k)], d[cols(k), :], preferred_element_type=F32)

        each(rows // tile, part)

    def base(k):
        load_w(k).wait()

        def part(t):
            at = pl.ds(pl.multiple_of(t * tile, tile), tile)
            acc[at, :] += jnp.dot(x[at, cols(k)], w[cols(k), :], preferred_element_type=F32)

        each(rows // tile, part)

    def step(i, carry):
        @pl.when(i + AHEAD < CHUNKS)
        def _():
            own_z(i + AHEAD)

        @pl.when(i + AHEAD_Y < CHUNKS)
        def _():
            own_y(i + AHEAD_Y)

        @pl.when(i < CHUNKS)
        def _():
            def from_z(j):
                zz = lax.rem(z + 1 + j, nz)
                arrived(i, place(zz, y, c))
                if near:

                    @pl.when(((z == 1) | (z == 2)) & (zz == 6 - 3 * z))
                    def _():
                        relay(i, lambda t: t.start())

                each(ny - 1, lambda t: to_y(i, zz, t).start())

            each(nz - 1, from_z)
            to_s(i, y).start()

        @pl.when((i >= LAG_Y) & (i < CHUNKS + LAG_Y))
        def _():
            def from_y(t):
                yy = lax.rem(y + 1 + t, ny)
                each(nz, lambda zz: arrived(i - LAG_Y, place(zz, yy, c)))
                to_s(i - LAG_Y, yy).start()

            each(ny - 1, from_y)

        @pl.when(i >= LAG)
        def _():
            each(ny, lambda yy: from_s(i - LAG, yy))

            @pl.when(i == LAG)
            def _():
                each(lines - 1, lambda t: spread_to(*telling, t).start())

            @pl.when(i == LAG + 2)
            def _():
                each(lines - 1, lambda t: spread_from(*telling, t))
                across(*telling, c).start()

            down(i - LAG)

            @pl.when(i - LAG < CHUNKS - 1)
            def _():
                base(i - LAG)

        @pl.when(i == LAG + 3)
        def _():
            tables()

        return carry

    def tables():
        across(*telling, 1 - c).wait_recv()
        lane = lax.broadcasted_iota(jnp.int32, (block, 128), 1)
        sub = lax.broadcasted_iota(jnp.int32, (block, 128), 0)

        def ids(q):
            row = meta[pl.ds(q * 8, 1), :]
            col = jnp.sum(jnp.where(lane == sub, row, 0), axis=1, keepdims=True)
            idcol[pl.ds(pl.multiple_of(q * block, block), block), :] = jnp.broadcast_to(
                col, (block, 128)
            )

        each(pool, ids)

        def part(t):
            at = pl.ds(pl.multiple_of(t * tile, tile), tile)
            row = row_of(lax.broadcasted_iota(jnp.int32, (tile, 128), 0) + t * tile)

            def quad(q):
                parts = [meta[pl.ds((q * 4 + s) * 8 + 1, 1), :] for s in range(4)]
                for half in range(2):
                    line = jnp.concatenate(
                        [t[:, half * HALF : (half + 1) * HALF] for t in parts], axis=1
                    )
                    expand[half, at, pl.ds(pl.multiple_of(q * 128, 128), 128)] = jnp.where(
                        row == line, 1.0, 0.0
                    ).astype(BF16)

            each(pool // 4, quad)

        each(rows // tile, part)

    lax.fori_loop(0, CHUNKS + LAG, step, 0)

    own_list = meta[pl.ds(here * 8 + 1, 1), :]
    eye = lax.broadcasted_iota(jnp.int32, (SLOTS, 128), 0) == lax.broadcasted_iota(
        jnp.int32, (SLOTS, 128), 1
    )
    own_col = jnp.sum(jnp.where(eye, own_list, 0), axis=1, keepdims=True)
    pick = jnp.where(
        own_col == row_of(lax.broadcasted_iota(jnp.int32, (SLOTS, rows), 1)), 1.0, 0.0
    ).astype(BF16)
    low = jnp.dot(pick, accd[...].astype(BF16), preferred_element_type=F32)
    picked = jnp.dot(pick, idcol[...].astype(F32).astype(BF16), preferred_element_type=F32)
    slot = picked - (me * ADP_DEV).astype(F32)
    lane = lax.broadcasted_iota(jnp.int32, (SLOTS, 128), 1)
    low = jnp.where(slot == (lane // ADAPTER_RANK).astype(F32), low, 0.0)
    low = low[:, :ADAPTER_RANK] + low[:, ADAPTER_RANK:]
    mine_c = pl.ds(pl.multiple_of(here * HALF, HALF), HALF)
    comp[mine_c, :] = jnp.concatenate([low[:HALF], low[HALF:]], axis=1).astype(BF16)

    each(lines - 1, lambda i: spread_to(*sharing, i).start())
    base(CHUNKS - 1)
    load_u.wait()
    each(lines - 1, lambda i: spread_from(*sharing, i))
    across(*sharing, c).start()
    across(*sharing, 1 - c).wait_recv()

    def finish(t):
        at = pl.ds(pl.multiple_of(t * tile, tile), tile)
        first = jnp.dot(expand[0, at, :], comp[...], preferred_element_type=F32)
        second = jnp.dot(expand[1, at, :], comp[...], preferred_element_type=F32)
        factor = first[:, :ADAPTER_RANK] + second[:, ADAPTER_RANK:]
        pair = jnp.concatenate([factor, factor], axis=1).astype(BF16).astype(F32)
        ids = idcol[at, :] - lax.broadcasted_iota(jnp.int32, (tile, 128), 1) // ADAPTER_RANK
        for q in range(u.shape[0] // 128):
            wide[:, q * 128 : (q + 1) * 128] = jnp.where(ids == q * ADP_DEV, pair, 0.0).astype(BF16)
        delta = jnp.dot(wide[...], u[...], preferred_element_type=F32)
        result = (acc[at, :] + delta).astype(BF16)
        for s in range(tile // block):
            row = row_of((t * (tile // block) + s) * block)
            out_ref[pl.ds(pl.multiple_of(row, block), block), :] = result[s * block : (s + 1) * block]

    each(rows // tile, finish)

    def done(k):
        z_sends(k, lambda t: t.wait_send())
        if near:
            relay(k, lambda t: t.wait_send())
        for i in range(ny - 1):
            each(nz, lambda zz: to_y(k, zz, i).wait_send())
        for yy in range(ny):
            to_s(k, yy).wait_send()

    lax.fori_loop(0, CHUNKS, lambda k, t: (done(k), t)[1], 0)
    for what in (telling, sharing):
        each(lines - 1, lambda i: spread_to(*what, i).wait_send())
        across(*what, c).wait_send()


def local(nz, ny, hidden, gain, weight, down, up, ids, requests):
    pool = nz * ny * 2
    block, width = hidden.shape
    rows = block * pool
    n = weight.shape[1]
    tile = min(rows, 256)
    dma = pltpu.SemaphoreType.DMA
    vm = pl.BlockSpec(memory_space=pltpu.VMEM)
    hbm = pl.BlockSpec(memory_space=pl.ANY)
    return pl.pallas_call(
        functools.partial(kernel, nz, ny),
        out_shape=jax.ShapeDtypeStruct((rows, n), BF16),
        in_specs=[hbm, hbm, hbm, hbm, hbm, vm, vm],
        out_specs=vm,
        scratch_shapes=[
            pltpu.VMEM((rows, width), BF16),
            pltpu.VMEM(weight.shape, BF16),
            pltpu.VMEM(down.shape, BF16),
            pltpu.VMEM(up.shape, BF16),
            pltpu.VMEM((block, width), BF16),
            pltpu.VMEM((width,), BF16),
            pltpu.VMEM((rows, n), F32),
            pltpu.VMEM((rows, down.shape[1]), F32),
            pltpu.VMEM((pool * 8, 128), jnp.int32),
            pltpu.VMEM((pool * HALF, 128), BF16),
            pltpu.VMEM((2, rows, pool * HALF), BF16),
            pltpu.VMEM((rows, 128), jnp.int32),
            pltpu.VMEM((tile, up.shape[0]), BF16),
            dma,
            dma,
            dma((CHUNKS,)),
            dma((CHUNKS,)),
            dma,
            dma((CHUNKS, nz)),
            dma((CHUNKS, nz * max(ny - 1, 1))),
            dma((CHUNKS, ny)),
            dma((CHUNKS, pool)),
            dma((CHUNKS, ny)),
            dma((pool,)),
            dma((pool + 1,)),
            dma((pool,)),
            dma((pool + 1,)),
        ],
        compiler_params=pltpu.CompilerParams(
            collective_id=0, has_side_effects=True, vmem_limit_bytes=56 * 1024 * 1024
        ),
    )(hidden, gain, weight, down, up, ids, requests)


def solution(mesh):
    pool = mesh.shape["pool"]
    ny = 2 if pool == 16 else 1
    nz = pool // (2 * ny)
    return jax.shard_map(
        functools.partial(local, nz, ny),
        mesh=mesh,
        in_specs=(
            P(("groups", "pool"), None),
            P(),
            P(None, "pool"),
            P(None, ("groups", "pool")),
            P("groups", "pool"),
            P(("groups", "pool")),
            P(("groups", "pool")),
        ),
        out_specs=P("groups", "pool"),
        check_vma=False,
    )
```

time: 52.2 us -> 48 us (0.920)
  Pallas kernels: 48.8 us -> 45.6 us
  local copies, waits for them, and re-layouts: 3.02 us -> 1.67 us
    pallas_call x1, Pallas kernels: 48.8 us -> 45.6 us  [local(): pl.pallas_call(functools.partial(kernel, nz, ny), out_shape=jax.ShapeDtyp...]
    reshape x1 -> x0, local copies, waits for them, and re-layouts: 1.35 us -> none  [local(): gain.reshape(1, -1)]
where the time goes in v2:
time: 48 us; the launch traced here: 47.3 us
  Pallas kernels  45.6 us (95%)
  local copies, waits for them, and re-layouts  1.67 us (3%)
    pallas_call x1, Pallas kernels, local(): pl.pallas_call(functools.partial(kernel, nz, ny), out_shape=jax.ShapeDtyp...  45.6 us
    unnamed x1, local copies, waits for them, and re-layouts  1.67 us

profile of v2, /device:TPU:0, one launch (start us, length us, event | category | flops | bytes accessed | tf_op | source)
XLA Modules:
  0.0 47.3 jit_solution(3834493876824980232)
XLA Ops:
  0.0 45.6 %shard_map.73 = bf16[256,512]{1,0:T(8,128)(2,1)} custom-call(bf16[16,8192]{1,0:T(8,128)(2,1)} %h_hbm.1, bf16[8192]{0:T(1024)(128)(2,1)} %g_hbm.1, bf16[8192,512]{1,0:T(8,128)(2,1)} %w_hbm.1, bf16[8192,128]{1,0:T(8,128)(2,1)} %d_hbm.1, bf16[2048,512]{1,0:T(8,128)(2,1)} %u_hbm.1, s32[16]{0:T(128)} %ids_ref.1, s32[48]{0:T(128)} %list_ref.1), custom_call_target="tpu_custom_call" | custom-call | tf_op jit(solution)/shard_map/pallas_call | solution.py:383
  45.6 1.7 %copy.9 = bf16[256,512]{1,0:T(8,128)(2,1)} copy(bf16[256,512]{1,0:T(8,128)(2,1)} %shard_map.73) | data formatting | bytes 524288

commit v3 on v2

--- a/solution.py
+++ b/solution.py
@@ -20,6 +20,9 @@
 F32, BF16 = jnp.float32, jnp.bfloat16
 
 
+DEFER = 3
+
+
 def each(n, body):
     if n <= 8:
         for i in range(n):
@@ -36,7 +39,7 @@
 def kernel(
     nz, ny, h_hbm, g_hbm, w_hbm, d_hbm, u_hbm, ids_ref, list_ref, out_ref,
     x, w, d, u, h, g, acc, accd, meta, comp, expand, idcol, wide,
-    h_sem, g_sem, w_sem, d_sem, u_sem, z_send, y_send, s_send, recv, s_recv,
+    h_sem, g_sem, w_sem, d_sem, u_sem, z_send, p_send, y_send, s_send, recv, s_recv,
     m_send, m_recv, c_send, c_recv,
 ):
     pool = nz * ny * 2
@@ -136,7 +139,12 @@
         zz = lax.rem(z + 1 + i, nz)
         return to(z_send.at[k, i], recv.at[k, here], piece(here, k), pid(zz, y, c))
 
-    def z_sends(k, act):
+    def to_z_peer(k, i):
+        at = place(z, lax.rem(y + 1, ny), c)
+        zz = lax.rem(z + 1 + i, nz)
+        return to(p_send.at[i], recv.at[k, at], piece(at, k), pid(zz, y, c))
+
+    def z_sends(k, act, to_z=to_z):
         def one(i):
             if near:
 
@@ -148,11 +156,15 @@
 
         each(nz - 1, one)
 
-    def relay(k, act):
-        @pl.when((z == 1) | (z == 2))
-        def _():
-            at = place(6 - 3 * z, y, c)
-            act(to(z_send.at[k, nz - 1], recv.at[k, at], piece(at, k), pid(3 * z - 3, y, c)))
+    def relay(k, act, yy, sem):
+        at = place(6 - 3 * z, yy, c)
+        act(to(sem, recv.at[k, at], piece(at, k), pid(3 * z - 3, y, c)))
+
+    middle = (z == 1) | (z == 2)
+    both = ny == 2
+    last = CHUNKS - 1
+    regular = CHUNKS - 1 if both else CHUNKS
+    peer = lax.rem(y + 1, ny)
 
     def to_y(k, zz, i):
         at = place(zz, y, c)
@@ -181,6 +193,8 @@
             own_z(k)
         if k < AHEAD_Y:
             own_y(k)
+    if both:
+        own_y(last)
 
     acc[...] = jnp.zeros_like(acc)
     accd[...] = jnp.zeros_like(accd)
@@ -227,27 +241,52 @@
         def _():
             own_z(i + AHEAD)
 
-        @pl.when(i + AHEAD_Y < CHUNKS)
+        if both:
+
+            @pl.when(i + AHEAD == last)
+            def _():
+                arrived(last, place(z, peer, c))
+                z_sends(last, lambda t: t.start(), to_z_peer)
+
+        @pl.when(i + AHEAD_Y < regular)
         def _():
             own_y(i + AHEAD_Y)
 
-        @pl.when(i < CHUNKS)
+        @pl.when(i < regular)
         def _():
             def from_z(j):
                 zz = lax.rem(z + 1 + j, nz)
                 arrived(i, place(zz, y, c))
                 if near:
 
-                    @pl.when(((z == 1) | (z == 2)) & (zz == 6 - 3 * z))
+                    @pl.when(middle & (zz == 6 - 3 * z))
                     def _():
-                        relay(i, lambda t: t.start())
+                        relay(i, lambda t: t.start(), y, z_send.at[i, nz - 1])
 
                 each(ny - 1, lambda t: to_y(i, zz, t).start())
 
             each(nz - 1, from_z)
             to_s(i, y).start()
 
-        @pl.when((i >= LAG_Y) & (i < CHUNKS + LAG_Y))
+        if both:
+
+            @pl.when(i == last)
+            def _():
+                for yy, sem in ((y, z_send.at[last, nz - 1]), (peer, p_send.at[nz - 1])):
+
+                    def from_z(j):
+                        zz = lax.rem(z + 1 + j, nz)
+                        arrived(last, place(zz, yy, c))
+                        if near:
+
+                            @pl.when(middle & (zz == 6 - 3 * z))
+                            def _():
+                                relay(last, lambda t: t.start(), yy, sem)
+
+                    each(nz - 1, from_z)
+                    to_s(last, yy).start()
+
+        @pl.when((i >= LAG_Y) & (i < regular + LAG_Y))
         def _():
             def from_y(t):
                 yy = lax.rem(y + 1 + t, ny)
@@ -271,7 +310,7 @@
 
             down(i - LAG)
 
-            @pl.when(i - LAG < CHUNKS - 1)
+            @pl.when(i - LAG < CHUNKS - DEFER)
             def _():
                 base(i - LAG)
 
@@ -295,6 +334,7 @@
 
         each(pool, ids)
 
+    def one_hots():
         def part(t):
             at = pl.ds(pl.multiple_of(t * tile, tile), tile)
             row = row_of(lax.broadcasted_iota(jnp.int32, (tile, 128), 0) + t * tile)
@@ -333,7 +373,8 @@
     comp[mine_c, :] = jnp.concatenate([low[:HALF], low[HALF:]], axis=1).astype(BF16)
 
     each(lines - 1, lambda i: spread_to(*sharing, i).start())
-    base(CHUNKS - 1)
+    lax.fori_loop(CHUNKS - DEFER, CHUNKS, lambda k, t: (base(k), t)[1], 0)
+    one_hots()
     load_u.wait()
     each(lines - 1, lambda i: spread_from(*sharing, i))
     across(*sharing, c).start()
@@ -359,13 +400,29 @@
     def done(k):
         z_sends(k, lambda t: t.wait_send())
         if near:
-            relay(k, lambda t: t.wait_send())
-        for i in range(ny - 1):
-            each(nz, lambda zz: to_y(k, zz, i).wait_send())
+
+            @pl.when(middle)
+            def _():
+                relay(k, lambda t: t.wait_send(), y, z_send.at[k, nz - 1])
+
+        @pl.when(k < regular)
+        def _():
+            for i in range(ny - 1):
+                each(nz, lambda zz: to_y(k, zz, i).wait_send())
+
         for yy in range(ny):
             to_s(k, yy).wait_send()
 
     lax.fori_loop(0, CHUNKS, lambda k, t: (done(k), t)[1], 0)
+    if both:
+        each(ny - 1, lambda i: to_y(last, z, i).wait_send())
+        z_sends(last, lambda t: t.wait_send(), to_z_peer)
+        if near:
+
+            @pl.when(middle)
+            def _():
+                relay(last, lambda t: t.wait_send(), peer, p_send.at[nz - 1])
+
     for what in (telling, sharing):
         each(lines - 1, lambda i: spread_to(*what, i).wait_send())
         across(*what, c).wait_send()
@@ -405,6 +462,7 @@
             dma((CHUNKS,)),
             dma,
             dma((CHUNKS, nz)),
+            dma((nz,)),
             dma((CHUNKS, nz * max(ny - 1, 1))),
             dma((CHUNKS, ny)),
             dma((CHUNKS, pool)),

time: 48 us -> 45.8 us (0.954); the launches traced: 47.3 us -> 45.6 us
  Pallas kernels: 45.6 us -> 43.9 us
    pallas_call x1, Pallas kernels: 45.6 us -> 43.9 us  [local(): pl.pallas_call(functools.partial(kernel, nz, ny), out_shape=jax.ShapeDtyp...]
where the time goes in v3:
time: 45.8 us; the launch traced here: 45.6 us
  Pallas kernels  43.9 us (96%)
  local copies, waits for them, and re-layouts  1.67 us (4%)
    pallas_call x1, Pallas kernels, local(): pl.pallas_call(functools.partial(kernel, nz, ny), out_shape=jax.ShapeDtyp...  43.9 us
    unnamed x1, local copies, waits for them, and re-layouts  1.67 us

profile of v3, /device:TPU:0, one launch (start us, length us, event | category | flops | bytes accessed | tf_op | source)
XLA Modules:
  0.0 45.6 jit_solution(11399386467463928053)
XLA Ops:
  0.0 43.9 %shard_map.73 = bf16[256,512]{1,0:T(8,128)(2,1)} custom-call(bf16[16,8192]{1,0:T(8,128)(2,1)} %h_hbm.1, bf16[8192]{0:T(1024)(128)(2,1)} %g_hbm.1, bf16[8192,512]{1,0:T(8,128)(2,1)} %w_hbm.1, bf16[8192,128]{1,0:T(8,128)(2,1)} %d_hbm.1, bf16[2048,512]{1,0:T(8,128)(2,1)} %u_hbm.1, s32[16]{0:T(128)} %ids_ref.1, s32[48]{0:T(128)} %list_ref.1), custom_call_target="tpu_custom_call" | custom-call | tf_op jit(solution)/shard_map/pallas_call | solution.py:440
  43.9 1.7 %copy.9 = bf16[256,512]{1,0:T(8,128)(2,1)} copy(bf16[256,512]{1,0:T(8,128)(2,1)} %shard_map.73) | data formatting | bytes 524288

commit v4 on v3

--- a/solution.py
+++ b/solution.py
@@ -105,11 +105,6 @@
 
     load_h.wait()
     load_g.wait()
-    for k in range(CHUNKS):
-        load_d(k).start()
-        load_w(k).start()
-    load_u.start()
-
     total = jnp.zeros((block, 128), F32)
     for k in range(CHUNKS):
         v = h[:, k * kc : (k + 1) * kc].astype(F32)
@@ -195,6 +190,11 @@
             own_y(k)
     if both:
         own_y(last)
+
+    for k in range(CHUNKS):
+        load_d(k).start()
+        load_w(k).start()
+    load_u.start()
 
     acc[...] = jnp.zeros_like(acc)
     accd[...] = jnp.zeros_like(accd)

time: 45.8 us -> 45.6 us (level)
  no operation moved by 1% of the time
where the time goes in v4:
time: 45.6 us; the launch traced here: 45.5 us
  Pallas kernels  43.8 us (96%)
  local copies, waits for them, and re-layouts  1.67 us (4%)
    pallas_call x1, Pallas kernels, local(): pl.pallas_call(functools.partial(kernel, nz, ny), out_shape=jax.ShapeDtyp...  43.8 us
    unnamed x1, local copies, waits for them, and re-layouts  1.67 us

profile of v4, /device:TPU:0, one launch (start us, length us, event | category | flops | bytes accessed | tf_op | source)
XLA Modules:
  0.0 45.5 jit_solution(14521582995335593783)
XLA Ops:
  0.0 43.8 %shard_map.73 = bf16[256,512]{1,0:T(8,128)(2,1)} custom-call(bf16[16,8192]{1,0:T(8,128)(2,1)} %h_hbm.1, bf16[8192]{0:T(1024)(128)(2,1)} %g_hbm.1, bf16[8192,512]{1,0:T(8,128)(2,1)} %w_hbm.1, bf16[8192,128]{1,0:T(8,128)(2,1)} %d_hbm.1, bf16[2048,512]{1,0:T(8,128)(2,1)} %u_hbm.1, s32[16]{0:T(128)} %ids_ref.1, s32[48]{0:T(128)} %list_ref.1), custom_call_target="tpu_custom_call" | custom-call | tf_op jit(solution)/shard_map/pallas_call | solution.py:440
  43.8 1.7 %copy.9 = bf16[256,512]{1,0:T(8,128)(2,1)} copy(bf16[256,512]{1,0:T(8,128)(2,1)} %shard_map.73) | data formatting | bytes 524288
